TPU v7x, 32 devices: a whole 2x2x4 slice. The times are simulated.
32 devices in a mesh: groups: 2 (over y), seq: 4 (over z), dp: 4 (over x, core).
Axes of the slice: x: 2, y: 2, z: 4, core: 2. Of those that a mesh axis runs over, the one named last changes fastest.
Arguments:
- inputs: bfloat16 [8, 65536, 512], P(('groups', 'dp'), 'seq'), parts along dimension 0, may hold values from -6 to 6
- cotangent: bfloat16 [8, 65536, 512], P(('groups', 'dp'), 'seq'), parts along dimension 0, may hold values from -6 to 6
- first_factor: bfloat16 [256, 256, 256], P('seq', 'dp'), may hold values from -0.375 to 0.375
- second_factor: bfloat16 [256, 256, 256], P('seq', 'dp'), may hold values from -0.375 to 0.375
Outputs:
- mixed_out: bfloat16 [8, 65536, 512], P(('groups', 'dp'), 'seq'), parts along dimension 0
- input_grad: bfloat16 [8, 65536, 512], P(('groups', 'dp'), 'seq'), parts along dimension 0
- first_factor_grad: bfloat16 [512, 256, 256], P(('groups', 'seq'), 'dp'), parts along dimension 0
- second_factor_grad: bfloat16 [512, 256, 256], P(('groups', 'seq'), 'dp'), parts along dimension 0
There are 2 independent parts, one for each index of `groups`. A program takes and returns all parts, laid end to end along the dimension named above; an argument that names none is the same for every part. Nothing has to cross between parts.
All inputs are finite; a program needn't handle non-finite values.
Results may differ from a plain program's by a relative error of at most 0.009.
Values may be sent and summed in bfloat16 or wider, within the bound.
A program may use at most 320 MiB of HBM per device.

v0:
```python
import math

import jax
import jax.numpy as jnp
from jax import lax
from jax.sharding import PartitionSpec as P


def silu_parts(values):
    sig = jax.nn.sigmoid(values)
    return (values * sig, sig * (1.0 + values * (1.0 - sig)))


def shards(inputs, cotangent, first_factor, second_factor):
    first_full, second_full = (
        lax.all_gather(first_factor, "dp", axis=1, tiled=True),
        lax.all_gather(second_factor, "dp", axis=1, tiled=True),
    )
    seqs_here = inputs.shape[0]
    rows_here = inputs.shape[1]
    channels = inputs.shape[2]
    blocks_here = first_full.shape[0]
    block_width = first_full.shape[1]
    columns_here = second_full.shape[0]
    second_width = second_full.shape[1]
    norm_scale = 1.0 / math.sqrt(lax.axis_size("dp") * seqs_here * channels)
    blocked = inputs.reshape(seqs_here, blocks_here, block_width, channels)
    first_out = jnp.einsum(
        "ijk,bikc->bijc", first_full, blocked, preferred_element_type=jnp.float32
    ).astype(jnp.bfloat16)
    exchanged = lax.all_to_all(first_out, "seq", split_axis=2, concat_axis=1, tiled=True)
    result = jnp.einsum(
        "jik,bkjc->bjic", second_full, exchanged, preferred_element_type=jnp.float32
    )
    mixing, exchanged = (result, exchanged)
    mixing = mixing.reshape(seqs_here, rows_here, channels)
    gate_value, gate_slope = silu_parts(inputs.astype(jnp.float32))
    outputs = (mixing * gate_value).astype(jnp.bfloat16)
    cot_f32 = cotangent.astype(jnp.float32)
    gated_cot = (
        (cot_f32 * gate_value)
        .astype(jnp.bfloat16)
        .reshape(seqs_here, columns_here, second_width, channels)
    )
    grad_two = norm_scale * jnp.einsum(
        "bjic,bkjc->jik", gated_cot, exchanged, preferred_element_type=jnp.float32
    )
    back_sent = jnp.einsum(
        "jik,bjic->bkjc", second_full, gated_cot, preferred_element_type=jnp.float32
    ).astype(jnp.bfloat16)
    back_rows = lax.all_to_all(back_sent, "seq", split_axis=1, concat_axis=2, tiled=True)
    grad_one = norm_scale * jnp.einsum(
        "bijc,bikc->ijk", back_rows, blocked, preferred_element_type=jnp.float32
    )
    local_grad = jnp.einsum(
        "ijk,bijc->bikc", first_full, back_rows, preferred_element_type=jnp.float32
    )
    input_grad = (
        local_grad.reshape(seqs_here, rows_here, channels) + cot_f32 * mixing * gate_slope
    ).astype(jnp.bfloat16)
    first_sum, second_sum = (
        lax.psum_scatter(
            grad_one.astype(jnp.bfloat16), "dp", scatter_dimension=1, tiled=True
        ).astype(jnp.float32),
        lax.psum_scatter(
            grad_two.astype(jnp.bfloat16), "dp", scatter_dimension=1, tiled=True
        ).astype(jnp.float32),
    )
    return (outputs, input_grad, first_sum.astype(jnp.bfloat16), second_sum.astype(jnp.bfloat16))


def solution(mesh):
    in_specs = (
        P(("groups", "dp"), "seq", None),
        P(("groups", "dp"), "seq", None),
        P("seq", "dp", None),
        P("seq", "dp", None),
    )
    out_specs = (
        P(("groups", "dp"), "seq", None),
        P(("groups", "dp"), "seq", None),
        P(("groups", "seq"), "dp", None),
        P(("groups", "seq"), "dp", None),
    )
    return jax.shard_map(shards, mesh=mesh, in_specs=in_specs, out_specs=out_specs, check_vma=False)
```

profile of v0, /device:TPU:0, one launch (start us, length us, event | category | flops | bytes accessed | tf_op | source)
XLA Modules:
  0.0 976.6 jit_solution(17166616666703134738)
XLA Ops:
  7.2 0.0 all-gather.3.cloned.1.call-start
  7.2 0.7 all-gather.3.cloned.1.call-update
  7.9 62.7 %all-gather.3.cloned.1.call-done = bf16[64,256,256]{2,1,0:T(8,128)(2,1)} async-done(((bf16[64,64,256]{2,1,0:T(8,128)(2,1)}), bf16[64,256,256]{2,1,0:T(8,128)(2,1)}) %all-gather.3.cloned.1.call-update) | async-done | bytes 8388624 | tf_op jit(solution)/shard_map/all_gather | solution.py:16
  70.6 19.3 %convert_bitcast_fusion.1 = bf16[1,64,256,512]{2,3,1,0:T(8,128)(2,1)} fusion(bf16[64,256,512]{2,1,0:T(8,128)(2,1)} %bitcast.45, bf16[64,256,256]{2,1,0:T(8,128)(2,1)} %all-gather.3.cloned.1.call-done), kind=kOutput, calls=%fused_computation.19 | convolution fusion | flops 4303355904 | bytes 41943040 | tf_op jit(solution)/shard_map/ijk,bikc->bijc/dot_general | solution.py:28
  89.9 23.4 %copy.19 = bf16[1,64,256,512]{3,1,0,2:T(8,128)(2,1)} copy(bf16[1,64,256,512]{2,3,1,0:T(8,128)(2,1)} %convert_bitcast_fusion.1) | data formatting | bytes 33554432 | tf_op jit(solution)/shard_map/convert_element_type | solution.py:30
  113.3 7.0 all-to-all-start
  120.3 0.0 all-gather.5.cloned.1.call-start
  120.3 0.7 all-gather.5.cloned.1.call-update
  121.0 22.1 %fusion = bf16[1,16384,512]{2,1,0:T(8,128)(2,1)} fusion(bf16[1,16384,512]{2,1,0:T(8,128)(2,1)} %param.5, bf16[1,16384,512]{2,1,0:T(8,128)(2,1)} %param.4), kind=kLoop, calls=%fused_computation.5 | loop fusion | flops 67108864 | bytes 50331648 | tf_op jit(solution)/shard_map/convert_element_type | solution.py:42
  143.1 38.3 %all-gather.5.cloned.1.call-done = bf16[64,256,256]{2,1,0:T(8,128)(2,1)} async-done(((bf16[64,64,256]{2,1,0:T(8,128)(2,1)}), bf16[64,256,256]{2,1,0:T(8,128)(2,1)}) %all-gather.5.cloned.1.call-update) | async-done | bytes 8388624 | tf_op jit(solution)/shard_map/all_gather | solution.py:17
  181.5 16.4 %convert_bitcast_fusion = bf16[1,256,64,512]{1,3,2,0:T(8,128)(2,1)} fusion(bf16[64,256,512]{2,1,0:T(8,128)(2,1)} %bitcast.47, bf16[64,256,256]{2,1,0:T(8,128)(2,1)} %all-gather.5.cloned.1.call-done), kind=kOutput, calls=%fused_computation.18 | convolution fusion | flops 4303355904 | bytes 41943040 | tf_op jit(solution)/shard_map/jik,bjic->bkjc/dot_general | solution.py:48
  197.9 23.4 %copy.23 = bf16[1,256,64,512]{3,2,0,1:T(8,128)(2,1)} copy(bf16[1,256,64,512]{1,3,2,0:T(8,128)(2,1)} %convert_bitcast_fusion) | data formatting | bytes 33554432 | tf_op jit(solution)/shard_map/convert_element_type | solution.py:50
  221.3 262.6 %all-to-all-done = bf16[1,64,256,512]{3,1,0,2:T(8,128)(2,1)} async-done(((bf16[1,64,256,512]{3,1,0,2:T(8,128)(2,1)}), bf16[1,64,256,512]{3,1,0,2:T(8,128)(2,1)}, u32[]{:S(2)}, u32[]{:S(2)}) %all-to-all-start) | async-done | bytes 16777248 | tf_op jit(solution)/shard_map/all_to_all | solution.py:31
  483.8 7.1 all-to-all-start.1
  490.9 0.2 reduce-scatter.5.cloned.1.call-start
  491.2 12.1 %copy.20 = bf16[1,64,256,512]{3,2,1,0:T(8,128)(2,1)S(1)} copy(bf16[1,64,256,512]{3,1,0,2:T(8,128)(2,1)} %all-to-all-done) | data formatting | bytes 33554432 | tf_op jit(solution)/shard_map/all_to_all | solution.py:31
  503.3 21.2 %copy.21 = bf16[1,4,64,64,512]{4,2,1,3,0:T(8,128)(2,1)} copy(bf16[1,4,64,64,512]{4,3,1,2,0:T(8,128)(2,1)S(1)} %bitcast.53) | data formatting | bytes 33554432 | tf_op jit(solution)/shard_map/all_to_all | solution.py:31
  524.5 15.5 %multiply_convert_fusion = bf16[64,256,256]{2,1,0:T(8,128)(2,1)} fusion(bf16[64,256,512]{2,1,0:T(8,128)(2,1)} %bitcast.48, bf16[256,64,512]{2,0,1:T(8,128)(2,1)} %bitcast.49), kind=kOutput, calls=%fused_computation.16 | convolution fusion | flops 4303355904 | bytes 41943040 | tf_op jit(solution)/shard_map/bjic,bkjc->jik/dot_general | solution.py:45
  540.0 0.0 reduce-scatter.5.cloned.1.call-update
  540.0 0.3 reduce-scatter.3.cloned.1.call-start
  540.3 313.4 %all-to-all-done.1 = bf16[1,256,64,512]{3,2,0,1:T(8,128)(2,1)} async-done(((bf16[1,256,64,512]{3,2,0,1:T(8,128)(2,1)}), bf16[1,256,64,512]{3,2,0,1:T(8,128)(2,1)}, u32[]{:S(2)}, u32[]{:S(2)}) %all-to-all-start.1) | async-done | bytes 16777248 | tf_op jit(solution)/shard_map/all_to_all | solution.py:51
  853.7 14.1 %copy.24 = bf16[1,64,4,64,512]{4,3,2,1,0:T(8,128)(2,1)} copy(bf16[1,64,4,64,512]{4,3,1,2,0:T(8,128)(2,1)} %bitcast.13) | data formatting | bytes 33554432 | tf_op jit(solution)/shard_map/all_to_all | solution.py:51
  867.7 15.5 %multiply_convert_fusion.1 = bf16[64,256,256]{2,1,0:T(8,128)(2,1)} fusion(bf16[64,256,512]{2,1,0:T(8,128)(2,1)} %bitcast.51, bf16[64,256,512]{2,1,0:T(8,128)(2,1)} %bitcast.46), kind=kOutput, calls=%fused_computation.17 | convolution fusion | flops 4303355904 | bytes 41943040 | tf_op jit(solution)/shard_map/bijc,bikc->ijk/dot_general | solution.py:52
  883.2 0.0 reduce-scatter.3.cloned.1.call-update
  883.2 23.1 %fusion.10 = f32[64,512,256]{1,2,0:T(8,128)} fusion(bf16[64,256,512]{2,1,0:T(8,128)(2,1)} %bitcast.52, bf16[64,256,256]{2,1,0:T(8,128)(2,1)} %all-gather.3.cloned.1.call-done), kind=kOutput, calls=%fused_computation.20 | convolution fusion | flops 4294967296 | bytes 58720256 | tf_op jit(solution)/shard_map/ijk,bijc->bikc/dot_general | solution.py:55
  906.4 18.3 %fusion.11 = f32[64,512,256]{1,2,0:T(8,128)} fusion(bf16[64,256,256]{2,1,0:T(8,128)(2,1)} %all-gather.5.cloned.1.call-done, bf16[256,64,512]{2,0,1:T(8,128)(2,1)} %bitcast.50), kind=kOutput, calls=%fused_computation.21 | convolution fusion | flops 4294967296 | bytes 58720256 | tf_op jit(solution)/shard_map/jik,bkjc->bjic/dot_general | solution.py:32
  924.7 45.3 %fusion.3 = (bf16[1,16384,512]{2,1,0:T(8,128)(2,1)}, bf16[1,16384,512]{2,1,0:T(8,128)(2,1)}) fusion(bf16[1,16384,512]{2,1,0:T(8,128)(2,1)} %param.5, bf16[1,16384,512]{2,1,0:T(8,128)(2,1)} %param.4, f32[64,512,256]{1,2,0:T(8,128)} %fusion.10, f32[64,512,256]{1,2,0:T(8,128)} %fusion.11), kind=kLoop, calls=%fused_computation.8 | loop fusion | flops 134217728 | bytes 134217728 | tf_op jit(solution)/shard_map/convert_element_type | solution.py:60
  970.0 0.0 reduce-scatter.5.cloned.1.call-done
  970.0 0.0 reduce-scatter.3.cloned.1.call-done
Async XLA Ops:
  7.2 63.4 %all-gather.3.cloned.1.call-start = ((), (), s32[]{:S(2)}) async-start(), calls=%async_computation.4 | async-start | bytes 10485760 | tf_op jit(solution)/shard_map/all_gather | solution.py:16
  113.3 370.5 %all-to-all-start = ((bf16[1,64,256,512]{3,1,0,2:T(8,128)(2,1)}), bf16[1,64,256,512]{3,1,0,2:T(8,128)(2,1)}, u32[]{:S(2)}, u32[]{:S(2)}) async-start(bf16[1,64,256,512]{3,1,0,2:T(8,128)(2,1)} %copy.19), calls=%async_computation | async-start | bytes 33554432 | tf_op jit(solution)/shard_map/all_to_all | solution.py:31
  120.3 61.2 %all-gather.5.cloned.1.call-start = ((), (), s32[]{:S(2)}) async-start(), calls=%async_computation.5 | async-start | bytes 10485760 | tf_op jit(solution)/shard_map/all_gather | solution.py:17
  483.8 369.8 %all-to-all-start.1 = ((bf16[1,256,64,512]{3,2,0,1:T(8,128)(2,1)}), bf16[1,256,64,512]{3,2,0,1:T(8,128)(2,1)}, u32[]{:S(2)}, u32[]{:S(2)}) async-start(bf16[1,256,64,512]{3,2,0,1:T(8,128)(2,1)} %copy.23), calls=%async_computation.1 | async-start | bytes 33554432 | tf_op jit(solution)/shard_map/all_to_all | solution.py:51
  490.9 479.1 %reduce-scatter.5.cloned.1.call-start = ((), (), s32[]{:S(2)}) async-start(), calls=%async_computation.7 | async-start | bytes 10485760 | tf_op jit(solution)/shard_map/reduce_scatter | solution.py:65
  540.0 430.0 %reduce-scatter.3.cloned.1.call-start = ((), (), s32[]{:S(2)}) async-start(), calls=%async_computation.6 | async-start | bytes 10485760 | tf_op jit(solution)/shard_map/reduce_scatter | solution.py:62
Sparse Core Ops, SparseCore 0:
  9.6 60.9 all-gather.2
  122.7 58.7 all-gather.4
  540.2 71.9 reduce-scatter.4
  883.4 69.8 reduce-scatter.2
where the time goes:
time: 978 us; the launch traced here: 977 us
  waiting for transfers between devices  678 us (69%)
  matrix products  108 us (11%)
  local copies, waits for them, and re-layouts  94.3 us (10%)
  other arithmetic  67.4 us (7%)
  starting transfers between devices  14.6 us (1%)
  between operations  13.8 us (1%)
    all_to_all x1, waiting for transfers between devices, shards(): lax.all_to_all(back_sent, 'seq', split_axis=1, concat_axis=2, tiled=True)  313 us
    all_to_all x1, waiting for transfers between devices, shards(): lax.all_to_all(first_out, 'seq', split_axis=2, concat_axis=1, tiled=True)  263 us
    all_gather x1, waiting for transfers between devices, shards(): lax.all_gather(first_factor, 'dp', axis=1, tiled=True)  62.7 us
    convert_element_type x1, other arithmetic, shards(): input_grad = (local_grad.reshape(seqs_here, rows_here, channels) + cot_f3...  45.3 us
    all_gather x1, waiting for transfers between devices, shards(): lax.all_gather(second_factor, 'dp', axis=1, tiled=True)  38.3 us
    all_to_all x2, local copies, waits for them, and re-layouts, shards(): lax.all_to_all(first_out, 'seq', split_axis=2, concat_axis=1, tiled=True)  33.4 us
    convert_element_type x1, local copies, waits for them, and re-layouts, shards(): first_out = jnp.einsum('ijk,bikc->bijc', first_full, blocked, preferred_e...  23.4 us
    convert_element_type x1, local copies, waits for them, and re-layouts, shards(): back_sent = jnp.einsum('jik,bjic->bkjc', second_full, gated_cot, preferre...  23.4 us
  transfers between devices with their start and end apart: 6, of which 4 were waited for; matrix products, arithmetic and copies ran while one was open for 23% of the time, Pallas kernels for 0%

commit v1 on v0

v1 whole, which is shorter than its diff:
```python
import math

import jax
import jax.numpy as jnp
from jax import lax
from jax.experimental.layout import Layout, with_layout_constraint
from jax.sharding import PartitionSpec as P


def silu_parts(values):
    sig = jax.nn.sigmoid(values)
    return (values * sig, sig * (1.0 + values * (1.0 - sig)))


def row_major(value):
    return with_layout_constraint(value, Layout(tuple(range(value.ndim))))


def scatter_rows(parts):
    blocks, ring, rows, columns = parts.shape
    flat = parts.reshape(blocks, ring * rows, columns)
    kept = lax.psum_scatter(flat, "dp", scatter_dimension=1, tiled=True)
    return kept.reshape(blocks, kept.shape[1] // rows, rows, columns)


def shards(inputs, cotangent, first_factor, second_factor):
    f32, bf16 = jnp.float32, jnp.bfloat16
    seqs = inputs.shape[0]
    rows = inputs.shape[1]
    channels = inputs.shape[2]
    ring = lax.axis_size("seq")
    blocks = first_factor.shape[0]
    columns = second_factor.shape[0]
    width = first_factor.shape[2]
    width_two = second_factor.shape[2]
    norm_scale = 1.0 / math.sqrt(lax.axis_size("dp") * seqs * channels)
    chunks = math.gcd(4, math.gcd(blocks, columns))
    ic, jc = blocks // chunks, columns // chunks

    blocked = inputs.reshape(seqs, blocks, width, channels)
    cot_f32 = cotangent.astype(f32)
    gate_value, gate_slope = silu_parts(inputs.astype(f32))

    def after(value, *others):
        kept = lax.optimization_barrier((value,) + others)
        return kept[0], kept[1:]

    def exchange(part):
        return lax.all_to_all(part, "seq", split_axis=0, concat_axis=0, tiled=True)

    first_parts, received = [], []
    for q in range(chunks):
        own = slice(q * ic, (q + 1) * ic)
        factor = lax.all_gather(first_factor[own], "dp", axis=1, tiled=True)
        first_parts.append(factor)
        part = jnp.einsum(
            "ijk,bikc->bijc", factor, blocked[:, own], preferred_element_type=f32
        ).astype(bf16)
        part = part.reshape(seqs, ic, ring, columns, channels).transpose(2, 0, 1, 3, 4)
        part = row_major(part)
        if q:
            part, (received[-1],) = after(part, received[-1])
        received.append(exchange(part))

    second_full = lax.all_gather(second_factor, "dp", axis=1, tiled=True)
    gated_cot = (
        (cot_f32 * gate_value).astype(bf16).reshape(seqs, columns, width_two, channels)
    )
    previous = received
    returned = []
    first_full = jnp.concatenate(first_parts, axis=0)
    first_split = first_full.reshape(blocks, ring, chunks, jc, width)

    def through_first(q, total):
        back = returned[q]
        grad_one = norm_scale * jnp.einsum(
            "sbitc,bikc->istk", back, blocked, preferred_element_type=f32
        )
        total = total + jnp.einsum(
            "istk,sbitc->bikc", first_split[:, :, q], back, preferred_element_type=f32
        )
        return grad_one.astype(bf16), total

    grads_one = []
    done = 0
    for q in range(chunks):
        own = slice(q * jc, (q + 1) * jc)
        part = jnp.einsum(
            "jik,bjic->bkjc", second_full[own], gated_cot[:, own], preferred_element_type=f32
        ).astype(bf16)
        part = part.reshape(seqs, ring, blocks, jc, channels).transpose(1, 0, 2, 3, 4)
        part = row_major(part)
        if q == chunks // 2:
            exchanged = jnp.concatenate(received, axis=2).transpose(1, 0, 2, 3, 4)
            exchanged = exchanged.reshape(seqs, ring * blocks, columns, channels)
            mixing = jnp.einsum(
                "jik,bkjc->bjic", second_full, exchanged, preferred_element_type=f32
            ).reshape(seqs, rows, channels)
            outputs = (mixing * gate_value).astype(bf16)
            grad_two = norm_scale * jnp.einsum(
                "bjic,bkjc->jik", gated_cot, exchanged, preferred_element_type=f32
            )
            grad_two = grad_two.astype(bf16)
            total = (cot_f32 * mixing * gate_slope).reshape(blocked.shape)
            part, (outputs, grad_two, total) = after(part, outputs, grad_two, total)
            second_sum = lax.psum_scatter(
                grad_two, "dp", scatter_dimension=1, tiled=True
            )
        elif q > chunks // 2:
            while done < q - 1:
                grad_one, total = through_first(done, total)
                grads_one.append(grad_one)
                done += 1
            part, (total, *grads_one) = after(part, total, *grads_one)
            grads_one = list(grads_one)
        part, (previous[-1],) = after(part, previous[-1])
        returned.append(exchange(part))
        previous = returned

    while done < chunks - 1:
        grad_one, total = through_first(done, total)
        grads_one.append(grad_one)
        done += 1
    first_sums = []
    if grads_one:
        early = jnp.concatenate(grads_one, axis=2)
        early_sum = scatter_rows(early)
        returned[-1], (early_sum, total, second_sum) = after(
            returned[-1], early_sum, total, second_sum
        )
        first_sums.append(early_sum)
    grad_one, total = through_first(chunks - 1, total)
    first_sums.append(scatter_rows(grad_one))
    first_sum = jnp.concatenate(first_sums, axis=2).reshape(first_factor.shape)
    input_grad = total.reshape(seqs, rows, channels).astype(bf16)
    return (outputs, input_grad, first_sum, second_sum)


def solution(mesh):
    in_specs = (
        P(("groups", "dp"), "seq", None),
        P(("groups", "dp"), "seq", None),
        P("seq", "dp", None),
        P("seq", "dp", None),
    )
    out_specs = (
        P(("groups", "dp"), "seq", None),
        P(("groups", "dp"), "seq", None),
        P(("groups", "seq"), "dp", None),
        P(("groups", "seq"), "dp", None),
    )
    return jax.shard_map(shards, mesh=mesh, in_specs=in_specs, out_specs=out_specs, check_vma=False)
```

time: 978 us -> 960 us (0.982)
  waiting for transfers between devices: 678 us -> 456 us
  matrix products: 108 us -> 250 us
  starting transfers between devices: 14.6 us -> 40.7 us
  other arithmetic: 67.4 us -> 88.4 us
    all_to_all x2 -> x8, waiting for transfers between devices: 576 us -> 404 us  [exchange(): return lax.all_to_all(part, 'seq', split_axis=0, concat_axis=0, tiled=True)]
    dot_general x4 -> x16, matrix products: 74.3 us -> 175 us  [the longest x4 98.4 us: through_first(): jnp.einsum('istk,sbitc->bikc', first_split[:, :, q], back, preferred_elem...]
    all_gather x2 -> x5, waiting for transfers between devices: 101 us -> 50 us  [the longest x4 50 us: shards(): factor = lax.all_gather(first_factor[own], 'dp', axis=1, tiled=True)]
    all_to_all x3 -> x0, local copies, waits for them, and re-layouts: 47.4 us -> none  [the longest x2 33.4 us: shards(): lax.all_to_all(first_out, 'seq', split_axis=2, concat_axis=1, tiled=True)]
    convert_element_type x2 -> x1, other arithmetic: 67.4 us -> 21.3 us  [shards(): (cot_f32 * gate_value).astype(bf16)]
    mul x0 -> x1, other arithmetic: none -> 40.1 us  [shards(): total = (cot_f32 * mixing * gate_slope).reshape(blocked.shape)]
    optimization_barrier x0 -> x1, local copies, waits for them, and re-layouts: none -> 33.7 us  [after(): kept = lax.optimization_barrier((value,) + others)]
    dot_general x1, matrix products: 18.3 us -> 51.6 us  [shards(): jnp.einsum('jik,bkjc->bjic', second_full, exchanged, preferred_element_ty...]
  transfers between devices with their start and end apart: 6 -> 16, of which waited for: 4 -> 9; matrix products, arithmetic and copies ran while one was open for 23% -> 43% of each run, Pallas kernels for 0% -> 0%
where the time goes in v1:
time: 960 us; the launch traced here: 952 us
  waiting for transfers between devices  456 us (48%)
  matrix products  250 us (26%)
  local copies, waits for them, and re-layouts  101 us (11%)
  other arithmetic  88.4 us (9%)
  starting transfers between devices  40.7 us (4%)
  between operations  14.9 us (2%)
    all_to_all x8, waiting for transfers between devices, exchange(): return lax.all_to_all(part, 'seq', split_axis=0, concat_axis=0, tiled=True)  404 us
    dot_general x4, matrix products, through_first(): jnp.einsum('istk,sbitc->bikc', first_split[:, :, q], back, preferred_elem...  98.4 us
    dot_general x1, matrix products, shards(): jnp.einsum('jik,bkjc->bjic', second_full, exchanged, preferred_element_ty...  51.6 us
    all_gather x4, waiting for transfers between devices, shards(): factor = lax.all_gather(first_factor[own], 'dp', axis=1, tiled=True)  50 us
    dot_general x4, matrix products, through_first(): jnp.einsum('sbitc,bikc->istk', back, blocked, preferred_element_type=f32)  43.1 us
    mul x1, other arithmetic, shards(): total = (cot_f32 * mixing * gate_slope).reshape(blocked.shape)  40.1 us
    all_to_all x8, starting transfers between devices, exchange(): return lax.all_to_all(part, 'seq', split_axis=0, concat_axis=0, tiled=True)  40 us
    optimization_barrier x1, local copies, waits for them, and re-layouts, after(): kept = lax.optimization_barrier((value,) + others)  33.7 us
  transfers between devices with their start and end apart: 16, of which 9 were waited for; matrix products, arithmetic and copies ran while one was open for 43% of the time, Pallas kernels for 0%

profile of v1, /device:TPU:0, one launch (start us, length us, event | category | flops | bytes accessed | tf_op | source)
XLA Modules:
  0.0 951.7 jit_solution(6830200255525887186)
XLA Ops:
  7.2 2.9 fusion.55
  10.1 25.4 %all-gather.10.cloned.1.call-done = bf16[16,256,256]{2,1,0:T(8,128)(2,1)} async-done(((bf16[16,64,256]{2,1,0:T(8,128)(2,1)}), bf16[16,256,256]{2,1,0:T(8,128)(2,1)}) %all-gather.10.cloned.1.call-update) | async-done | bytes 2097168 | tf_op jit(solution)/shard_map/all_gather | solution.py:54
  35.6 4.1 fusion.33
  41.9 4.9 all-to-all-start
  48.3 24.6 %all-gather.8.cloned.1.call-done = bf16[16,256,256]{2,1,0:T(8,128)(2,1)} async-done(((bf16[16,64,256]{2,1,0:T(8,128)(2,1)}), bf16[16,256,256]{2,1,0:T(8,128)(2,1)}) %all-gather.8.cloned.1.call-update) | async-done | bytes 2097168 | tf_op jit(solution)/shard_map/all_gather | solution.py:54
  72.8 4.1 fusion.32
  79.2 61.5 %all-to-all-done = bf16[4,1,16,64,512]{4,3,2,1,0:T(8,128)(2,1)} async-done(((bf16[4,1,16,64,512]{4,3,2,1,0:T(8,128)(2,1)}), bf16[4,1,16,64,512]{4,3,2,1,0:T(8,128)(2,1)}, u32[]{:S(2)}, u32[]{:S(2)}) %all-to-all-start) | async-done | bytes 4194336 | tf_op jit(solution)/shard_map/all_to_all | solution.py:49
  140.7 5.0 all-to-all-start.1
  148.9 4.1 fusion.34
  155.2 83.5 %all-to-all-done.1 = bf16[4,1,16,64,512]{4,3,2,1,0:T(8,128)(2,1)} async-done(((bf16[4,1,16,64,512]{4,3,2,1,0:T(8,128)(2,1)}), bf16[4,1,16,64,512]{4,3,2,1,0:T(8,128)(2,1)}, u32[]{:S(2)}, u32[]{:S(2)}) %all-to-all-start.1) | async-done | bytes 4194336 | tf_op jit(solution)/shard_map/all_to_all | solution.py:49
  238.8 4.8 all-to-all-start.2
  243.6 4.1 fusion.35
  250.0 86.3 %all-to-all-done.2 = bf16[4,1,16,64,512]{4,3,2,1,0:T(8,128)(2,1)} async-done(((bf16[4,1,16,64,512]{4,3,2,1,0:T(8,128)(2,1)}), bf16[4,1,16,64,512]{4,3,2,1,0:T(8,128)(2,1)}, u32[]{:S(2)}, u32[]{:S(2)}) %all-to-all-start.2) | async-done | bytes 4194336 | tf_op jit(solution)/shard_map/all_to_all | solution.py:49
  336.3 5.1 all-to-all-start.3
  341.3 21.3 %fusion = bf16[1,16384,512]{2,1,0:T(8,128)(2,1)} fusion(bf16[1,16384,512]{2,1,0:T(8,128)(2,1)} %param.5, bf16[1,16384,512]{2,1,0:T(8,128)(2,1)} %param.4), kind=kLoop, calls=%fused_computation.5 | loop fusion | flops 67108864 | bytes 50331648 | tf_op jit(solution)/shard_map/convert_element_type | solution.py:67
  362.6 5.3 fusion.54
  367.9 4.5 copy-done
  372.4 4.2 convert_bitcast_fusion.2
  376.7 4.3 copy.64
  383.6 4.4 copy.58
  388.0 46.1 %all-to-all-done.3 = bf16[4,1,16,64,512]{4,3,2,1,0:T(8,128)(2,1)} async-done(((bf16[4,1,16,64,512]{4,3,2,1,0:T(8,128)(2,1)}), bf16[4,1,16,64,512]{4,3,2,1,0:T(8,128)(2,1)}, u32[]{:S(2)}, u32[]{:S(2)}) %all-to-all-start.3) | async-done | bytes 4194336 | tf_op jit(solution)/shard_map/all_to_all | solution.py:49
  434.0 4.8 all-to-all-start.4
  439.3 14.0 %pad_maximum_fusion = bf16[4,1,64,64,512]{4,3,2,1,0:T(8,128)(2,1)} fusion(bf16[4,1,16,64,512]{4,3,2,1,0:T(8,128)(2,1)} %all-to-all-done.3, bf16[4,1,16,64,512]{4,3,2,1,0:T(8,128)(2,1)} %all-to-all-done.2, bf16[4,1,16,64,512]{4,3,2,1,0:T(8,128)(2,1)} %all-to-all-done.1, bf16[4,1,16,64,512]{4,3,2,1,0:T(8,128)(2,1)} %all-to-all-done), kind=kLoop, calls=%fused_computation.19 | loop fusion | flops 25165824 | bytes 33554432 | tf_op jit(solution)/shard_map/concatenate | solution.py:94
  453.3 51.6 %fusion.11 = f32[64,512,256]{1,2,0:T(8,128)} fusion(bf16[256,64,512]{2,1,0:T(8,128)(2,1)} %bitcast.197, bf16[64,256,256]{2,0,1:T(8,128)(2,1)} %all-gather.6.cloned.1.call-done), kind=kOutput, calls=%fused_computation.23 | convolution fusion | flops 4294967296 | bytes 58720256 | tf_op jit(solution)/shard_map/jik,bkjc->bjic/dot_general | solution.py:96
  504.9 40.1 %fusion.1 = (f32[1,16384,512]{2,1,0:T(8,128)}, bf16[1,16384,512]{2,1,0:T(8,128)(2,1)}) fusion(bf16[1,16384,512]{2,1,0:T(8,128)(2,1)} %param.5, bf16[1,16384,512]{2,1,0:T(8,128)(2,1)} %param.4, f32[64,512,256]{1,2,0:T(8,128)} %fusion.11), kind=kLoop, calls=%fused_computation.6 | loop fusion | flops 117440512 | bytes 117440512 | tf_op jit(solution)/shard_map/mul | solution.py:104
  545.0 24.3 %multiply_convert_fusion = bf16[64,256,256]{2,1,0:T(8,128)(2,1)} fusion(bf16[64,256,512]{2,1,0:T(8,128)(2,1)} %bitcast.199, bf16[256,64,512]{2,1,0:T(8,128)(2,1)} %bitcast.198), kind=kOutput, calls=%fused_computation.20 | convolution fusion | flops 4303355904 | bytes 41943040 | tf_op jit(solution)/shard_map/bjic,bkjc->jik/dot_general | solution.py:100
  569.3 4.8 convert_bitcast_fusion
  574.1 4.8 copy.71
  578.9 5.5 all-to-all-start.5
  584.4 4.1 pad_maximum_fusion.1
  591.4 5.1 convert_bitcast_fusion.1
  596.5 4.3 copy.69
  600.8 33.7 %copy.73 = f32[1,64,256,512]{2,3,1,0:T(8,128)} copy(f32[1,64,256,512]{3,2,1,0:T(8,128)} %bitcast.196) | data formatting | bytes 67108864 | tf_op jit(solution)/shard_map/optimization_barrier | solution.py:45
  634.6 17.9 %fusion.36 = f32[64,512,256,1]{2,1,0,3:T(8,128)} fusion(bf16[64,4,1,16,256]{4,3,2,1,0:T(8,128)(2,1)S(1)} %get-tuple-element.61, bf16[4,1,64,16,512]{4,3,2,1,0:T(8,128)(2,1)} %all-to-all-done.4), kind=kOutput, calls=%fused_computation.73 | convolution fusion | flops 1073741824 | bytes 39845888 | tf_op jit(solution)/shard_map/istk,sbitc->bikc/dot_general | solution.py:79
  652.4 24.2 %all-to-all-done.5 = bf16[4,1,64,16,512]{4,3,2,1,0:T(8,128)(2,1)} async-done(((bf16[4,1,64,16,512]{4,3,2,1,0:T(8,128)(2,1)}), bf16[4,1,64,16,512]{4,3,2,1,0:T(8,128)(2,1)}, u32[]{:S(2)}, u32[]{:S(2)}) %all-to-all-start.5) | async-done | bytes 4194336 | tf_op jit(solution)/shard_map/all_to_all | solution.py:49
  676.7 4.9 all-to-all-start.6
  681.6 10.2 %multiply_convert_fusion.4 = bf16[64,4,16,256]{3,2,1,0:T(8,128)(2,1)S(1)} fusion(bf16[64,256,512,1]{2,1,3,0:T(8,128)(2,1)} %bitcast.192, bf16[4,1,64,16,512]{4,3,2,1,0:T(8,128)(2,1)} %all-to-all-done.4), kind=kOutput, calls=%fused_computation.59 | convolution fusion | flops 1075838976 | bytes 23068672 | tf_op jit(solution)/shard_map/sbitc,bikc->istk/dot_general | solution.py:76
  691.8 11.3 %multiply_convert_fusion.3 = bf16[64,4,16,256]{3,2,1,0:T(8,128)(2,1)} fusion(bf16[64,256,512,1]{2,1,3,0:T(8,128)(2,1)} %bitcast.193, bf16[4,1,64,16,512]{4,3,2,1,0:T(8,128)(2,1)} %all-to-all-done.5), kind=kOutput, calls=%fused_computation.58 | convolution fusion | flops 1075838976 | bytes 23068672 | tf_op jit(solution)/shard_map/sbitc,bikc->istk/dot_general | solution.py:76
  703.1 35.8 %bitcast_add_fusion.2 = f32[1,64,256,512]{2,3,1,0:T(8,128)} fusion(f32[1,64,256,512]{2,3,1,0:T(8,128)} %copy.73, f32[64,512,256,1]{2,1,0,3:T(8,128)} %fusion.36, bf16[64,4,1,16,256]{4,3,2,1,0:T(8,128)(2,1)} %get-tuple-element.60, bf16[4,1,64,16,512]{4,3,2,1,0:T(8,128)(2,1)} %all-to-all-done.5), kind=kOutput, calls=%fused_computation.15 | convolution fusion | flops 1090519040 | bytes 106954752 | tf_op jit(solution)/shard_map/istk,sbitc->bikc/dot_general | solution.py:79
  738.9 35.3 %all-to-all-done.6 = bf16[4,1,64,16,512]{4,3,2,1,0:T(8,128)(2,1)} async-done(((bf16[4,1,64,16,512]{4,3,2,1,0:T(8,128)(2,1)}), bf16[4,1,64,16,512]{4,3,2,1,0:T(8,128)(2,1)}, u32[]{:S(2)}, u32[]{:S(2)}) %all-to-all-start.6) | async-done | bytes 4194336 | tf_op jit(solution)/shard_map/all_to_all | solution.py:49
  774.2 10.1 %multiply_convert_fusion.2 = bf16[64,4,16,256]{3,2,1,0:T(8,128)(2,1)S(1)} fusion(bf16[64,256,512,1]{2,1,3,0:T(8,128)(2,1)} %bitcast.194, bf16[4,1,64,16,512]{4,3,2,1,0:T(8,128)(2,1)} %all-to-all-done.6), kind=kOutput, calls=%fused_computation.57 | convolution fusion | flops 1075838976 | bytes 23068672 | tf_op jit(solution)/shard_map/sbitc,bikc->istk/dot_general | solution.py:76
  784.4 6.3 pad_maximum_fusion.2
  790.7 5.0 all-to-all-start.7
  795.7 25.4 %bitcast_add_fusion.1 = f32[1,64,256,512]{2,3,1,0:T(8,128)} fusion(f32[1,64,256,512]{2,3,1,0:T(8,128)} %bitcast_add_fusion.2, bf16[64,4,1,16,256]{4,3,2,1,0:T(8,128)(2,1)S(1)} %copy-done.2, bf16[4,1,64,16,512]{4,3,2,1,0:T(8,128)(2,1)} %all-to-all-done.6), kind=kOutput, calls=%fused_computation.14 | convolution fusion | flops 1082130432 | bytes 73400320 | tf_op jit(solution)/shard_map/istk,sbitc->bikc/dot_general | solution.py:79
  821.2 67.2 %all-to-all-done.7 = bf16[4,1,64,16,512]{4,3,2,1,0:T(8,128)(2,1)} async-done(((bf16[4,1,64,16,512]{4,3,2,1,0:T(8,128)(2,1)}), bf16[4,1,64,16,512]{4,3,2,1,0:T(8,128)(2,1)}, u32[]{:S(2)}, u32[]{:S(2)}) %all-to-all-start.7) | async-done | bytes 4194336 | tf_op jit(solution)/shard_map/all_to_all | solution.py:49
  888.4 11.5 %multiply_convert_fusion.1 = bf16[64,4,16,256]{3,2,1,0:T(8,128)(2,1)} fusion(bf16[64,256,512,1]{2,1,3,0:T(8,128)(2,1)} %bitcast.195, bf16[4,1,64,16,512]{4,3,2,1,0:T(8,128)(2,1)} %all-to-all-done.7), kind=kOutput, calls=%fused_computation.56 | convolution fusion | flops 1075838976 | bytes 23068672 | tf_op jit(solution)/shard_map/sbitc,bikc->istk/dot_general | solution.py:76
  899.9 19.3 %fusion.7 = bf16[1,64,256,512]{2,3,1,0:T(8,128)(2,1)} fusion(f32[1,64,256,512]{2,3,1,0:T(8,128)} %bitcast_add_fusion.1, bf16[64,4,1,16,256]{4,3,2,1,0:T(8,128)(2,1)S(1)} %copy-done.6, bf16[4,1,64,16,512]{4,3,2,1,0:T(8,128)(2,1)} %all-to-all-done.7), kind=kOutput, calls=%fused_computation.13 | convolution fusion | flops 1090519040 | bytes 56623104 | tf_op jit(solution)/shard_map/istk,sbitc->bikc/dot_general | solution.py:79
  919.2 22.6 %copy.81 = bf16[1,64,256,512]{3,2,1,0:T(8,128)(2,1)} copy(bf16[1,64,256,512]{2,3,1,0:T(8,128)(2,1)} %fusion.7) | data formatting | bytes 33554432 | tf_op jit(solution)/shard_map/convert_element_type | solution.py:135
  (46 shorter events, 22.5 us)
Async XLA Ops:
  7.2 28.4 %all-gather.10.cloned.1.call-start = ((), (), s32[]{:S(2)}) async-start(), calls=%async_computation.13 | async-start | bytes 2621440 | tf_op jit(solution)/shard_map/all_gather | solution.py:54
  41.9 98.8 %all-to-all-start = ((bf16[4,1,16,64,512]{4,3,2,1,0:T(8,128)(2,1)}), bf16[4,1,16,64,512]{4,3,2,1,0:T(8,128)(2,1)}, u32[]{:S(2)}, u32[]{:S(2)}) async-start(bf16[4,1,16,64,512]{4,3,2,1,0:T(8,128)(2,1)} %bitcast.212), calls=%async_computation | async-start | bytes 8388608 | tf_op jit(solution)/shard_map/all_to_all | solution.py:49
  46.8 26.0 %all-gather.8.cloned.1.call-start = ((), (), s32[]{:S(2)}) async-start(), calls=%async_computation.12 | async-start | bytes 2621440 | tf_op jit(solution)/shard_map/all_gather | solution.py:54
  47.6 101.3 %all-gather.12.cloned.1.call-start = ((), (), s32[]{:S(2)}) async-start(), calls=%async_computation.14 | async-start | bytes 2621440 | tf_op jit(solution)/shard_map/all_gather | solution.py:54
  140.7 5.6 copy-start.5
  140.7 98.1 %all-to-all-start.1 = ((bf16[4,1,16,64,512]{4,3,2,1,0:T(8,128)(2,1)}), bf16[4,1,16,64,512]{4,3,2,1,0:T(8,128)(2,1)}, u32[]{:S(2)}, u32[]{:S(2)}) async-start(bf16[4,1,16,64,512]{4,3,2,1,0:T(8,128)(2,1)} %bitcast.211), calls=%async_computation.1 | async-start | bytes 8388608 | tf_op jit(solution)/shard_map/all_to_all | solution.py:49
  145.7 97.9 %all-gather.14.cloned.1.call-start = ((), (), s32[]{:S(2)}) async-start(), calls=%async_computation.15 | async-start | bytes 2621440 | tf_op jit(solution)/shard_map/all_gather | solution.py:54
  146.3 216.3 %all-gather.6.cloned.1.call-start = ((), (), s32[]{:S(2)}) async-start(), calls=%async_computation.11 | async-start | bytes 10485760 | tf_op jit(solution)/shard_map/all_gather | solution.py:65
  238.8 97.5 %all-to-all-start.2 = ((bf16[4,1,16,64,512]{4,3,2,1,0:T(8,128)(2,1)}), bf16[4,1,16,64,512]{4,3,2,1,0:T(8,128)(2,1)}, u32[]{:S(2)}, u32[]{:S(2)}) async-start(bf16[4,1,16,64,512]{4,3,2,1,0:T(8,128)(2,1)} %bitcast.215), calls=%async_computation.2 | async-start | bytes 8388608 | tf_op jit(solution)/shard_map/all_to_all | solution.py:49
  336.3 97.7 %all-to-all-start.3 = ((bf16[4,1,16,64,512]{4,3,2,1,0:T(8,128)(2,1)}), bf16[4,1,16,64,512]{4,3,2,1,0:T(8,128)(2,1)}, u32[]{:S(2)}, u32[]{:S(2)}) async-start(bf16[4,1,16,64,512]{4,3,2,1,0:T(8,128)(2,1)} %bitcast.214), calls=%async_computation.3 | async-start | bytes 8388608 | tf_op jit(solution)/shard_map/all_to_all | solution.py:49
  362.6 9.8 %copy-start = (bf16[1,16384,512]{2,1,0:T(8,128)(2,1)S(1)}, bf16[1,16384,512]{2,1,0:T(8,128)(2,1)}, u32[]{:S(2)}) copy-start(bf16[1,16384,512]{2,1,0:T(8,128)(2,1)} %fusion) | copy-start | bytes 50331652
  434.0 144.8 %all-to-all-start.4 = ((bf16[4,1,64,16,512]{4,3,2,1,0:T(8,128)(2,1)}), bf16[4,1,64,16,512]{4,3,2,1,0:T(8,128)(2,1)}, u32[]{:S(2)}, u32[]{:S(2)}) async-start(bf16[4,1,64,16,512]{4,3,2,1,0:T(8,128)(2,1)} %bitcast.210), calls=%async_computation.4 | async-start | bytes 8388608 | tf_op jit(solution)/shard_map/all_to_all | solution.py:49
  438.9 382.3 %reduce-scatter.6.cloned.1.call-start = ((), (), s32[]{:S(2)}) async-start(), calls=%async_computation.17 | async-start | bytes 10485760 | tf_op jit(solution)/shard_map/reduce_scatter | solution.py:106
  578.9 5.5 copy-start.3
  578.9 97.8 %all-to-all-start.5 = ((bf16[4,1,64,16,512]{4,3,2,1,0:T(8,128)(2,1)}), bf16[4,1,64,16,512]{4,3,2,1,0:T(8,128)(2,1)}, u32[]{:S(2)}, u32[]{:S(2)}) async-start(bf16[4,1,64,16,512]{4,3,2,1,0:T(8,128)(2,1)} %bitcast.213), calls=%async_computation.5 | async-start | bytes 8388608 | tf_op jit(solution)/shard_map/all_to_all | solution.py:49
  588.5 2.9 copy-start.4
  676.7 97.6 %all-to-all-start.6 = ((bf16[4,1,64,16,512]{4,3,2,1,0:T(8,128)(2,1)}), bf16[4,1,64,16,512]{4,3,2,1,0:T(8,128)(2,1)}, u32[]{:S(2)}, u32[]{:S(2)}) async-start(bf16[4,1,64,16,512]{4,3,2,1,0:T(8,128)(2,1)} %bitcast.208), calls=%async_computation.6 | async-start | bytes 8388608 | tf_op jit(solution)/shard_map/all_to_all | solution.py:49
  681.5 206.8 %reduce-scatter.4.cloned.1.call-start = ((), (), s32[]{:S(2)}) async-start(), calls=%async_computation.16 | async-start | bytes 7864320 | tf_op jit(solution)/shard_map/reduce_scatter | solution.py:22
  774.2 10.1 %copy-start.1 = (bf16[64,4,16,256]{3,2,1,0:T(8,128)(2,1)S(1)}, bf16[64,4,16,256]{3,2,1,0:T(8,128)(2,1)}, u32[]{:S(2)}) copy-start(bf16[64,4,16,256]{3,2,1,0:T(8,128)(2,1)} %multiply_convert_fusion.3) | copy-start | bytes 6291460
  790.7 5.1 copy-start.2
  790.7 97.7 %all-to-all-start.7 = ((bf16[4,1,64,16,512]{4,3,2,1,0:T(8,128)(2,1)}), bf16[4,1,64,16,512]{4,3,2,1,0:T(8,128)(2,1)}, u32[]{:S(2)}, u32[]{:S(2)}) async-start(bf16[4,1,64,16,512]{4,3,2,1,0:T(8,128)(2,1)} %bitcast.209), calls=%async_computation.7 | async-start | bytes 8388608 | tf_op jit(solution)/shard_map/all_to_all | solution.py:49
  795.7 146.1 %reduce-scatter.8.cloned.1.call-start = ((), (), s32[]{:S(2)}) async-start(), calls=%async_computation.18 | async-start | bytes 2621440 | tf_op jit(solution)/shard_map/reduce_scatter | solution.py:22
  888.4 11.5 %copy-start.6 = (bf16[64,4,1,16,256]{4,3,2,1,0:T(8,128)(2,1)S(1)}, bf16[64,4,1,16,256]{4,3,2,1,0:T(8,128)(2,1)}, u32[]{:S(2)}) copy-start(bf16[64,4,1,16,256]{4,3,2,1,0:T(8,128)(2,1)} %get-tuple-element.58) | copy-start | bytes 6291460
  919.2 22.6 %copy-start.7 = (bf16[64,48,256]{2,1,0:T(8,128)(2,1)S(1)}, bf16[64,48,256]{2,1,0:T(8,128)(2,1)}, u32[]{:S(2)}) copy-start(bf16[64,48,256]{2,1,0:T(8,128)(2,1)} %reduce-scatter.4.cloned.1.call-done) | copy-start | bytes 4718596
Sparse Core Ops, SparseCore 0:
  10.2 25.2 all-gather.9
  49.8 23.0 all-gather.7
  74.4 22.5 all-gather.11
  147.8 23.0 all-gather.13
  172.8 58.2 all-gather.5
  569.4 72.1 reduce-scatter.5
  790.8 56.5 reduce-scatter.3
  900.0 29.5 reduce-scatter.7

commit v2 on v1

--- a/solution.py
+++ b/solution.py
@@ -3,13 +3,53 @@
 import jax
 import jax.numpy as jnp
 from jax import lax
+from jax.experimental import pallas as pl
 from jax.experimental.layout import Layout, with_layout_constraint
+from jax.experimental.pallas import tpu as pltpu
 from jax.sharding import PartitionSpec as P
 
 
 def silu_parts(values):
     sig = jax.nn.sigmoid(values)
     return (values * sig, sig * (1.0 + values * (1.0 - sig)))
+
+
+def add_back(total, factors, backs, out_type):
+    blocks, width, channels = total.shape
+    step = math.gcd(blocks, 4)
+    count = len(backs)
+
+    def kernel(*refs):
+        total_ref, out_ref = refs[0], refs[-1]
+        factor_refs, back_refs = refs[1 : 1 + count], refs[1 + count : 1 + 2 * count]
+        for block in range(step):
+            value = total_ref[block]
+            for factor_ref, back_ref in zip(factor_refs, back_refs):
+                sources = back_ref.shape[0]
+                left = jnp.concatenate([factor_ref[block, n] for n in range(sources)], axis=0)
+                right = jnp.concatenate([back_ref[n, block] for n in range(sources)], axis=0)
+                value = value + lax.dot_general(
+                    left, right, (((0,), (0,)), ((), ())), preferred_element_type=jnp.float32
+                )
+            out_ref[block] = value.astype(out_ref.dtype)
+
+    whole = pl.BlockSpec((step, width, channels), lambda n: (n, 0, 0))
+    sources, _, rows, _ = backs[0].shape
+    return pl.pallas_call(
+        kernel,
+        grid=(blocks // step,),
+        in_specs=[whole]
+        + [pl.BlockSpec((step, sources, rows, width), lambda n: (n, 0, 0, 0))] * count
+        + [pl.BlockSpec((sources, step, rows, channels), lambda n: (0, n, 0, 0))] * count,
+        out_specs=whole,
+        out_shape=jax.ShapeDtypeStruct(total.shape, out_type),
+        compiler_params=pltpu.CompilerParams(vmem_limit_bytes=40 * 1024 * 1024),
+        cost_estimate=pl.CostEstimate(
+            flops=2 * count * blocks * sources * rows * width * channels,
+            bytes_accessed=blocks * width * channels * 8,
+            transcendentals=0,
+        ),
+    )(total, *factors, *backs)
 
 
 def row_major(value):
@@ -71,18 +111,22 @@
     first_full = jnp.concatenate(first_parts, axis=0)
     first_split = first_full.reshape(blocks, ring, chunks, jc, width)
 
-    def through_first(q, total):
-        back = returned[q]
+    def grad_of(q):
         grad_one = norm_scale * jnp.einsum(
-            "sbitc,bikc->istk", back, blocked, preferred_element_type=f32
+            "sbitc,bikc->istk", returned[q], blocked, preferred_element_type=f32
         )
-        total = total + jnp.einsum(
-            "istk,sbitc->bikc", first_split[:, :, q], back, preferred_element_type=f32
-        )
-        return grad_one.astype(bf16), total
+        return grad_one.astype(bf16)
 
-    grads_one = []
-    done = 0
+    def through_first(some, total, out_type):
+        factors = [first_split[:, :, q] for q in some]
+        backs = [returned[q].reshape(ring, blocks, jc, channels) for q in some]
+        if jc % 16:
+            factors = [f.reshape(blocks, 1, ring * jc, width) for f in factors]
+            backs = [
+                g.transpose(1, 0, 2, 3).reshape(1, blocks, ring * jc, channels) for g in backs
+            ]
+        return add_back(total, factors, backs, out_type)
+
     for q in range(chunks):
         own = slice(q * jc, (q + 1) * jc)
         part = jnp.einsum(
@@ -96,43 +140,38 @@
             mixing = jnp.einsum(
                 "jik,bkjc->bjic", second_full, exchanged, preferred_element_type=f32
             ).reshape(seqs, rows, channels)
+            mixing, (exchanged, returned[0]) = after(mixing, exchanged, returned[0])
             outputs = (mixing * gate_value).astype(bf16)
             grad_two = norm_scale * jnp.einsum(
                 "bjic,bkjc->jik", gated_cot, exchanged, preferred_element_type=f32
             )
             grad_two = grad_two.astype(bf16)
-            total = (cot_f32 * mixing * gate_slope).reshape(blocked.shape)
+            total = (cot_f32 * mixing * gate_slope).reshape(blocks, width, channels)
             part, (outputs, grad_two, total) = after(part, outputs, grad_two, total)
             second_sum = lax.psum_scatter(
                 grad_two, "dp", scatter_dimension=1, tiled=True
             )
-        elif q > chunks // 2:
-            while done < q - 1:
-                grad_one, total = through_first(done, total)
-                grads_one.append(grad_one)
-                done += 1
-            part, (total, *grads_one) = after(part, total, *grads_one)
-            grads_one = list(grads_one)
         part, (previous[-1],) = after(part, previous[-1])
         returned.append(exchange(part))
         previous = returned
 
-    while done < chunks - 1:
-        grad_one, total = through_first(done, total)
-        grads_one.append(grad_one)
-        done += 1
-    first_sums = []
-    if grads_one:
-        early = jnp.concatenate(grads_one, axis=2)
-        early_sum = scatter_rows(early)
-        returned[-1], (early_sum, total, second_sum) = after(
-            returned[-1], early_sum, total, second_sum
-        )
-        first_sums.append(early_sum)
-    grad_one, total = through_first(chunks - 1, total)
-    first_sums.append(scatter_rows(grad_one))
-    first_sum = jnp.concatenate(first_sums, axis=2).reshape(first_factor.shape)
-    input_grad = total.reshape(seqs, rows, channels).astype(bf16)
+    last = chunks - 1
+    total = through_first(range(last - 1), total, f32)
+    sums = []
+    for q in range(last - 1):
+        early = grad_of(q)
+        if sums:
+            early, (sums[-1],) = after(early, sums[-1])
+        sums.append(scatter_rows(early))
+    total = through_first([last - 1], total, f32)
+    middle = grad_of(last - 1)
+    returned[last], (total, middle, second_sum, *sums) = after(
+        returned[last], total, middle, second_sum, *sums
+    )
+    grad_one = grad_of(last)
+    sums.append(scatter_rows(jnp.concatenate([middle, grad_one], axis=2)))
+    first_sum = jnp.concatenate(sums, axis=2).reshape(first_factor.shape)
+    input_grad = through_first([last], total, bf16).reshape(seqs, rows, channels)
     return (outputs, input_grad, first_sum, second_sum)
 
 

time: 960 us -> 910 us (0.948)
  matrix products: 250 us -> 156 us
  Pallas kernels: 0 us -> 86.5 us
  local copies, waits for them, and re-layouts: 101 us -> 57.4 us
  waiting for transfers between devices: 456 us -> 477 us
  other arithmetic: 88.4 us -> 71 us
    dot_general x8 -> x4, matrix products: 141 us -> 44.1 us  [grad_of(): jnp.einsum('sbitc,bikc->istk', returned[q], blocked, preferred_element_ty...]
    pallas_call x0 -> x3, Pallas kernels: none -> 86.5 us  [add_back(): pl.pallas_call(kernel, grid=(blocks // step,), in_specs=[whole] + [pl.Blo...]
    optimization_barrier x1 -> x0, local copies, waits for them, and re-layouts: 33.7 us -> none  [after(): kept = lax.optimization_barrier((value,) + others)]
    convert_element_type x1 -> x0, local copies, waits for them, and re-layouts: 22.6 us -> none  [shards(): input_grad = total.reshape(seqs, rows, channels).astype(bf16)]
    reduce_scatter x2 -> x3, waiting for transfers between devices: 0.01 us -> 17.8 us  [scatter_rows(): kept = lax.psum_scatter(flat, 'dp', scatter_dimension=1, tiled=True)]
    concatenate x2 -> x1, other arithmetic: 20.3 us -> 2.59 us  [shards(): sums.append(scatter_rows(jnp.concatenate([middle, grad_one], axis=2)))]
    unnamed x17 -> x18, local copies, waits for them, and re-layouts: 7.03 us -> 16.8 us
  transfers between devices with their start and end apart: 16 -> 17, of which waited for: 9 -> 11; matrix products, arithmetic and copies ran while one was open for 43% -> 29% of each run, Pallas kernels for 0% -> 10%
where the time goes in v2:
time: 910 us; the launch traced here: 902 us
  waiting for transfers between devices  477 us (52%)
  matrix products  156 us (17%)
  Pallas kernels  86.5 us (10%)
  other arithmetic  71 us (8%)
  local copies, waits for them, and re-layouts  57.4 us (6%)
  starting transfers between devices  40.6 us (4%)
  between operations  14.5 us (2%)
    all_to_all x8, waiting for transfers between devices, exchange(): return lax.all_to_all(part, 'seq', split_axis=0, concat_axis=0, tiled=True)  406 us
    pallas_call x3, Pallas kernels, add_back(): pl.pallas_call(kernel, grid=(blocks // step,), in_specs=[whole] + [pl.Blo...  86.5 us
    dot_general x1, matrix products, shards(): jnp.einsum('jik,bkjc->bjic', second_full, exchanged, preferred_element_ty...  51.7 us
    all_gather x4, waiting for transfers between devices, shards(): factor = lax.all_gather(first_factor[own], 'dp', axis=1, tiled=True)  50 us
    dot_general x4, matrix products, grad_of(): jnp.einsum('sbitc,bikc->istk', returned[q], blocked, preferred_element_ty...  44.1 us
    mul x1, other arithmetic, shards(): total = (cot_f32 * mixing * gate_slope).reshape(blocks, width, channels)  40.3 us
    all_to_all x8, starting transfers between devices, exchange(): return lax.all_to_all(part, 'seq', split_axis=0, concat_axis=0, tiled=True)  40.3 us
    dot_general x1, matrix products, shards(): jnp.einsum('bjic,bkjc->jik', gated_cot, exchanged, preferred_element_type...  24.2 us
  transfers between devices with their start and end apart: 17, of which 11 were waited for; matrix products, arithmetic and copies ran while one was open for 29% of the time, Pallas kernels for 10%

profile of v2, /device:TPU:0, one launch (start us, length us, event | category | flops | bytes accessed | tf_op | source)
XLA Modules:
  0.0 902.5 jit_solution(13435356080774764599)
XLA Ops:
  10.1 25.4 %all-gather.10.cloned.1.call-done = bf16[16,256,256]{2,1,0:T(8,128)(2,1)} async-done(((bf16[16,64,256]{2,1,0:T(8,128)(2,1)}), bf16[16,256,256]{2,1,0:T(8,128)(2,1)}) %all-gather.10.cloned.1.call-update) | async-done | bytes 2097168 | tf_op jit(solution)/shard_map/all_gather | solution.py:94
  35.6 4.1 fusion.32
  42.0 4.9 all-to-all-start
  48.3 24.6 %all-gather.8.cloned.1.call-done = bf16[16,256,256]{2,1,0:T(8,128)(2,1)} async-done(((bf16[16,64,256]{2,1,0:T(8,128)(2,1)}), bf16[16,256,256]{2,1,0:T(8,128)(2,1)}) %all-gather.8.cloned.1.call-update) | async-done | bytes 2097168 | tf_op jit(solution)/shard_map/all_gather | solution.py:94
  72.9 4.1 fusion.31
  79.2 61.5 %all-to-all-done = bf16[4,1,16,64,512]{4,3,2,1,0:T(8,128)(2,1)} async-done(((bf16[4,1,16,64,512]{4,3,2,1,0:T(8,128)(2,1)}), bf16[4,1,16,64,512]{4,3,2,1,0:T(8,128)(2,1)}, u32[]{:S(2)}, u32[]{:S(2)}) %all-to-all-start) | async-done | bytes 4194336 | tf_op jit(solution)/shard_map/all_to_all | solution.py:89
  140.7 5.0 all-to-all-start.1
  148.9 4.1 fusion.33
  155.3 83.5 %all-to-all-done.1 = bf16[4,1,16,64,512]{4,3,2,1,0:T(8,128)(2,1)} async-done(((bf16[4,1,16,64,512]{4,3,2,1,0:T(8,128)(2,1)}), bf16[4,1,16,64,512]{4,3,2,1,0:T(8,128)(2,1)}, u32[]{:S(2)}, u32[]{:S(2)}) %all-to-all-start.1) | async-done | bytes 4194336 | tf_op jit(solution)/shard_map/all_to_all | solution.py:89
  238.8 4.8 all-to-all-start.2
  243.7 4.1 fusion.34
  250.0 86.3 %all-to-all-done.2 = bf16[4,1,16,64,512]{4,3,2,1,0:T(8,128)(2,1)} async-done(((bf16[4,1,16,64,512]{4,3,2,1,0:T(8,128)(2,1)}), bf16[4,1,16,64,512]{4,3,2,1,0:T(8,128)(2,1)}, u32[]{:S(2)}, u32[]{:S(2)}) %all-to-all-start.2) | async-done | bytes 4194336 | tf_op jit(solution)/shard_map/all_to_all | solution.py:89
  336.3 5.1 all-to-all-start.3
  341.4 21.3 %fusion = bf16[1,16384,512]{2,1,0:T(8,128)(2,1)} fusion(bf16[1,16384,512]{2,1,0:T(8,128)(2,1)} %param.5, bf16[1,16384,512]{2,1,0:T(8,128)(2,1)} %param.4), kind=kLoop, calls=%fused_computation.5 | loop fusion | flops 67108864 | bytes 50331648 | tf_op jit(solution)/shard_map/convert_element_type | solution.py:107
  362.7 5.2 fusion.47
  367.8 4.8 convert_bitcast_fusion.2
  372.6 4.3 copy.56
  376.9 57.1 %all-to-all-done.3 = bf16[4,1,16,64,512]{4,3,2,1,0:T(8,128)(2,1)} async-done(((bf16[4,1,16,64,512]{4,3,2,1,0:T(8,128)(2,1)}), bf16[4,1,16,64,512]{4,3,2,1,0:T(8,128)(2,1)}, u32[]{:S(2)}, u32[]{:S(2)}) %all-to-all-start.3) | async-done | bytes 4194336 | tf_op jit(solution)/shard_map/all_to_all | solution.py:89
  434.1 5.2 all-to-all-start.4
  439.4 4.8 constant_dynamic-update-slice_fusion.3
  444.2 4.8 convert_bitcast_fusion.1
  449.0 4.4 copy.60
  453.4 4.8 convert_bitcast_fusion.3
  458.2 4.3 copy.50
  462.5 4.7 constant_dynamic-update-slice_fusion.2
  467.2 4.7 constant_dynamic-update-slice_fusion.1
  471.9 4.7 constant_dynamic-update-slice_fusion
  476.6 51.7 %fusion.10 = f32[64,512,256]{1,2,0:T(8,128)} fusion(bf16[256,64,512]{2,1,0:T(8,128)(2,1)} %bitcast.30, bf16[64,256,256]{2,0,1:T(8,128)(2,1)} %all-gather.6.cloned.1.call-done), kind=kOutput, calls=%fused_computation.16 | convolution fusion | flops 4294967296 | bytes 58720256 | tf_op jit(solution)/shard_map/jik,bkjc->bjic/dot_general | solution.py:140
  528.3 3.7 all-to-all-done.4
  532.0 4.8 all-to-all-start.5
  536.9 11.5 %multiply_convert_fusion.3 = bf16[64,4,16,256]{3,2,1,0:T(8,128)(2,1)} fusion(bf16[64,256,512,1]{2,1,3,0:T(8,128)(2,1)} %bitcast.168, bf16[4,1,64,16,512]{4,3,2,1,0:T(8,128)(2,1)} %all-to-all-done.4), kind=kOutput, calls=%fused_computation.51 | convolution fusion | flops 1075838976 | bytes 23068672 | tf_op jit(solution)/shard_map/sbitc,bikc->istk/dot_general | solution.py:115
  548.5 40.3 %fusion.1 = (f32[1,16384,512]{2,1,0:T(8,128)}, bf16[1,16384,512]{2,1,0:T(8,128)(2,1)}) fusion(f32[1,16384,512]{2,1,0:T(8,128)} %bitcast.172, bf16[1,16384,512]{2,1,0:T(8,128)(2,1)} %param.5, bf16[1,16384,512]{2,1,0:T(8,128)(2,1)} %param.4), kind=kLoop, calls=%fused_computation.6 | loop fusion | flops 117440512 | bytes 117440512 | tf_op jit(solution)/shard_map/mul | solution.py:149
  588.8 24.2 %multiply_convert_fusion.1 = bf16[64,256,256]{2,1,0:T(8,128)(2,1)} fusion(bf16[64,256,512]{2,1,0:T(8,128)(2,1)} %bitcast.177, bf16[1,256,64,512]{3,2,1,0:T(8,128)(2,1)} %bitcast.34), kind=kOutput, calls=%fused_computation.18 | convolution fusion | flops 4303355904 | bytes 41943040 | tf_op jit(solution)/shard_map/bjic,bkjc->jik/dot_general | solution.py:145
  613.1 16.5 %all-to-all-done.5 = bf16[4,1,64,16,512]{4,3,2,1,0:T(8,128)(2,1)} async-done(((bf16[4,1,64,16,512]{4,3,2,1,0:T(8,128)(2,1)}), bf16[4,1,64,16,512]{4,3,2,1,0:T(8,128)(2,1)}, u32[]{:S(2)}, u32[]{:S(2)}) %all-to-all-start.5) | async-done | bytes 4194336 | tf_op jit(solution)/shard_map/all_to_all | solution.py:89
  629.6 11.3 %multiply_convert_fusion.4 = bf16[64,4,16,256]{3,2,1,0:T(8,128)(2,1)} fusion(bf16[64,256,512,1]{2,1,3,0:T(8,128)(2,1)} %bitcast.169, bf16[4,1,64,16,512]{4,3,2,1,0:T(8,128)(2,1)} %all-to-all-done.5), kind=kOutput, calls=%fused_computation.52 | convolution fusion | flops 1075838976 | bytes 23068672 | tf_op jit(solution)/shard_map/sbitc,bikc->istk/dot_general | solution.py:115
  641.6 5.4 all-to-all-start.6
  647.0 5.0 convert_bitcast_fusion
  652.0 4.4 copy.63
  656.3 83.1 %all-to-all-done.6 = bf16[4,1,64,16,512]{4,3,2,1,0:T(8,128)(2,1)} async-done(((bf16[4,1,64,16,512]{4,3,2,1,0:T(8,128)(2,1)}), bf16[4,1,64,16,512]{4,3,2,1,0:T(8,128)(2,1)}, u32[]{:S(2)}, u32[]{:S(2)}) %all-to-all-start.6) | async-done | bytes 4194336 | tf_op jit(solution)/shard_map/all_to_all | solution.py:89
  739.4 5.0 all-to-all-start.7
  744.5 4.0 pad_maximum_fusion
  749.8 32.0 %shard_map.75.refs_0_ = f32[64,256,512]{2,1,0:T(8,128)} custom-call(f32[64,256,512]{2,1,0:T(8,128)} %bitcast.173, bf16[64,4,16,256]{3,2,1,0:T(8,128)(2,1)S(1)} %get-tuple-element.67.refs_1_, bf16[64,4,16,256]{3,2,1,0:T(8,128)(2,1)S(1)} %get-tuple-element.66.refs_2_, bf16[4,64,16,512]{3,2,1,0:T(8,128)(2,1)} %bitcast.49.refs_3_, ...), custom_call_target="tpu_custom_call" | custom-call | flops 2147483648 | bytes 67108864 | tf_op jit(solution)/shard_map/pallas_call | solution.py:38
  781.7 29.5 %shard_map.76.refs_0_ = f32[64,256,512]{2,1,0:T(8,128)} custom-call(f32[64,256,512]{2,1,0:T(8,128)} %shard_map.75.refs_0_, bf16[64,4,16,256]{3,2,1,0:T(8,128)(2,1)S(1)} %get-tuple-element.65.refs_1_, bf16[4,64,16,512]{3,2,1,0:T(8,128)(2,1)} %bitcast.52.refs_2_), custom_call_target="tpu_custom_call" | custom-call | flops 1073741824 | bytes 67108864 | tf_op jit(solution)/shard_map/pallas_call | solution.py:38
  811.2 11.3 %multiply_convert_fusion.5 = bf16[64,4,16,256]{3,2,1,0:T(8,128)(2,1)} fusion(bf16[64,256,512,1]{2,1,3,0:T(8,128)(2,1)} %bitcast.170, bf16[4,1,64,16,512]{4,3,2,1,0:T(8,128)(2,1)} %all-to-all-done.6), kind=kOutput, calls=%fused_computation.53 | convolution fusion | flops 1075838976 | bytes 23068672 | tf_op jit(solution)/shard_map/sbitc,bikc->istk/dot_general | solution.py:115
  822.5 14.6 %all-to-all-done.7 = bf16[4,1,64,16,512]{4,3,2,1,0:T(8,128)(2,1)} async-done(((bf16[4,1,64,16,512]{4,3,2,1,0:T(8,128)(2,1)}), bf16[4,1,64,16,512]{4,3,2,1,0:T(8,128)(2,1)}, u32[]{:S(2)}, u32[]{:S(2)}) %all-to-all-start.7) | async-done | bytes 4194336 | tf_op jit(solution)/shard_map/all_to_all | solution.py:89
  837.2 10.1 %multiply_convert_fusion.2 = bf16[64,4,16,256]{3,2,1,0:T(8,128)(2,1)S(1)} fusion(bf16[64,256,512,1]{2,1,3,0:T(8,128)(2,1)} %bitcast.171, bf16[4,1,64,16,512]{4,3,2,1,0:T(8,128)(2,1)} %all-to-all-done.7), kind=kOutput, calls=%fused_computation.50 | convolution fusion | flops 1075838976 | bytes 23068672 | tf_op jit(solution)/shard_map/sbitc,bikc->istk/dot_general | solution.py:115
  849.9 25.0 %shard_map.77 = bf16[64,256,512]{2,1,0:T(8,128)(2,1)} custom-call(f32[64,256,512]{2,1,0:T(8,128)} %shard_map.76.refs_0_, bf16[64,4,16,256]{3,2,1,0:T(8,128)(2,1)S(1)} %get-tuple-element.64.refs_1_, bf16[4,64,16,512]{3,2,1,0:T(8,128)(2,1)} %bitcast.63.refs_2_), custom_call_target="tpu_custom_call" | custom-call | flops 1073741824 | bytes 67108864 | tf_op jit(solution)/shard_map/pallas_call | solution.py:38
  874.9 17.8 %reduce-scatter.11.cloned.1.call-done = bf16[64,32,256]{2,1,0:T(8,128)(2,1)} async-done(((bf16[64,128,256]{2,1,0:T(8,128)(2,1)}), bf16[64,32,256]{2,1,0:T(8,128)(2,1)}) %reduce-scatter.11.cloned.1.call-update) | async-done | bytes 1048592 | tf_op jit(solution)/shard_map/reduce_scatter | solution.py:62
  (47 shorter events, 24.3 us)
Async XLA Ops:
  7.2 28.4 %all-gather.10.cloned.1.call-start = ((), (), s32[]{:S(2)}) async-start(), calls=%async_computation.14 | async-start | bytes 2621440 | tf_op jit(solution)/shard_map/all_gather | solution.py:94
  42.0 98.8 %all-to-all-start = ((bf16[4,1,16,64,512]{4,3,2,1,0:T(8,128)(2,1)}), bf16[4,1,16,64,512]{4,3,2,1,0:T(8,128)(2,1)}, u32[]{:S(2)}, u32[]{:S(2)}) async-start(bf16[4,1,16,64,512]{4,3,2,1,0:T(8,128)(2,1)} %bitcast.187), calls=%async_computation | async-start | bytes 8388608 | tf_op jit(solution)/shard_map/all_to_all | solution.py:89
  46.8 26.0 %all-gather.8.cloned.1.call-start = ((), (), s32[]{:S(2)}) async-start(), calls=%async_computation.13 | async-start | bytes 2621440 | tf_op jit(solution)/shard_map/all_gather | solution.py:94
  47.6 101.3 %all-gather.12.cloned.1.call-start = ((), (), s32[]{:S(2)}) async-start(), calls=%async_computation.15 | async-start | bytes 2621440 | tf_op jit(solution)/shard_map/all_gather | solution.py:94
  140.7 5.6 copy-start.4
  140.7 98.1 %all-to-all-start.1 = ((bf16[4,1,16,64,512]{4,3,2,1,0:T(8,128)(2,1)}), bf16[4,1,16,64,512]{4,3,2,1,0:T(8,128)(2,1)}, u32[]{:S(2)}, u32[]{:S(2)}) async-start(bf16[4,1,16,64,512]{4,3,2,1,0:T(8,128)(2,1)} %bitcast.186), calls=%async_computation.1 | async-start | bytes 8388608 | tf_op jit(solution)/shard_map/all_to_all | solution.py:89
  145.7 97.9 %all-gather.14.cloned.1.call-start = ((), (), s32[]{:S(2)}) async-start(), calls=%async_computation.16 | async-start | bytes 2621440 | tf_op jit(solution)/shard_map/all_gather | solution.py:94
  146.3 216.4 %all-gather.6.cloned.1.call-start = ((), (), s32[]{:S(2)}) async-start(), calls=%async_computation.12 | async-start | bytes 10485760 | tf_op jit(solution)/shard_map/all_gather | solution.py:105
  238.8 97.5 %all-to-all-start.2 = ((bf16[4,1,16,64,512]{4,3,2,1,0:T(8,128)(2,1)}), bf16[4,1,16,64,512]{4,3,2,1,0:T(8,128)(2,1)}, u32[]{:S(2)}, u32[]{:S(2)}) async-start(bf16[4,1,16,64,512]{4,3,2,1,0:T(8,128)(2,1)} %bitcast.190), calls=%async_computation.2 | async-start | bytes 8388608 | tf_op jit(solution)/shard_map/all_to_all | solution.py:89
  336.3 97.8 %all-to-all-start.3 = ((bf16[4,1,16,64,512]{4,3,2,1,0:T(8,128)(2,1)}), bf16[4,1,16,64,512]{4,3,2,1,0:T(8,128)(2,1)}, u32[]{:S(2)}, u32[]{:S(2)}) async-start(bf16[4,1,16,64,512]{4,3,2,1,0:T(8,128)(2,1)} %bitcast.189), calls=%async_computation.3 | async-start | bytes 8388608 | tf_op jit(solution)/shard_map/all_to_all | solution.py:89
  434.1 97.9 %all-to-all-start.4 = ((bf16[4,1,64,16,512]{4,3,2,1,0:T(8,128)(2,1)}), bf16[4,1,64,16,512]{4,3,2,1,0:T(8,128)(2,1)}, u32[]{:S(2)}, u32[]{:S(2)}) async-start(bf16[4,1,64,16,512]{4,3,2,1,0:T(8,128)(2,1)} %bitcast.188), calls=%async_computation.4 | async-start | bytes 8388608 | tf_op jit(solution)/shard_map/all_to_all | solution.py:89
  439.3 4.9 copy-start.3
  449.0 4.4 copy-start.2
  532.0 97.5 %all-to-all-start.5 = ((bf16[4,1,64,16,512]{4,3,2,1,0:T(8,128)(2,1)}), bf16[4,1,64,16,512]{4,3,2,1,0:T(8,128)(2,1)}, u32[]{:S(2)}, u32[]{:S(2)}) async-start(bf16[4,1,64,16,512]{4,3,2,1,0:T(8,128)(2,1)} %bitcast.184), calls=%async_computation.5 | async-start | bytes 8388608 | tf_op jit(solution)/shard_map/all_to_all | solution.py:89
  536.9 104.0 %reduce-scatter.7.cloned.1.call-start = ((), (), s32[]{:S(2)}) async-start(), calls=%async_computation.18 | async-start | bytes 2621440 | tf_op jit(solution)/shard_map/reduce_scatter | solution.py:62
  548.5 274.1 %reduce-scatter.9.cloned.1.call-start = ((), (), s32[]{:S(2)}) async-start(), calls=%async_computation.19 | async-start | bytes 2621440 | tf_op jit(solution)/shard_map/reduce_scatter | solution.py:62
  640.9 181.7 %reduce-scatter.5.cloned.1.call-start = ((), (), s32[]{:S(2)}) async-start(), calls=%async_computation.17 | async-start | bytes 10485760 | tf_op jit(solution)/shard_map/reduce_scatter | solution.py:151
  641.6 97.8 %all-to-all-start.6 = ((bf16[4,1,64,16,512]{4,3,2,1,0:T(8,128)(2,1)}), bf16[4,1,64,16,512]{4,3,2,1,0:T(8,128)(2,1)}, u32[]{:S(2)}, u32[]{:S(2)}) async-start(bf16[4,1,64,16,512]{4,3,2,1,0:T(8,128)(2,1)} %bitcast.183), calls=%async_computation.6 | async-start | bytes 8388608 | tf_op jit(solution)/shard_map/all_to_all | solution.py:89
  739.4 5.1 copy-start.1
  739.4 97.7 %all-to-all-start.7 = ((bf16[4,1,64,16,512]{4,3,2,1,0:T(8,128)(2,1)}), bf16[4,1,64,16,512]{4,3,2,1,0:T(8,128)(2,1)}, u32[]{:S(2)}, u32[]{:S(2)}) async-start(bf16[4,1,64,16,512]{4,3,2,1,0:T(8,128)(2,1)} %bitcast.185), calls=%async_computation.7 | async-start | bytes 8388608 | tf_op jit(solution)/shard_map/all_to_all | solution.py:89
  744.5 148.2 %reduce-scatter.11.cloned.1.call-start = ((), (), s32[]{:S(2)}) async-start(), calls=%async_computation.20 | async-start | bytes 5242880 | tf_op jit(solution)/shard_map/reduce_scatter | solution.py:62
  837.2 10.1 %copy-start = (bf16[64,4,16,256]{3,2,1,0:T(8,128)(2,1)S(1)}, bf16[64,4,16,256]{3,2,1,0:T(8,128)(2,1)}, u32[]{:S(2)}) copy-start(bf16[64,4,16,256]{3,2,1,0:T(8,128)(2,1)} %multiply_convert_fusion.5) | copy-start | bytes 6291460
  849.9 42.8 %copy-start.5 = (bf16[64,16,256]{2,1,0:T(8,128)(2,1)S(1)}, bf16[64,16,256]{2,1,0:T(8,128)(2,1)}, u32[]{:S(2)}) copy-start(bf16[64,16,256]{2,1,0:T(8,128)(2,1)} %reduce-scatter.7.cloned.1.call-done) | copy-start | bytes 1572868
  849.9 42.8 %copy-start.6 = (bf16[64,16,256]{2,1,0:T(8,128)(2,1)S(1)}, bf16[64,16,256]{2,1,0:T(8,128)(2,1)}, u32[]{:S(2)}) copy-start(bf16[64,16,256]{2,1,0:T(8,128)(2,1)} %reduce-scatter.9.cloned.1.call-done) | copy-start | bytes 1572868
Sparse Core Ops, SparseCore 0:
  10.3 25.2 all-gather.9
  49.8 23.0 all-gather.7
  74.5 22.5 all-gather.11
  148.4 23.0 all-gather.13
  173.4 58.2 all-gather.5
  548.6 31.8 reduce-scatter.6
  641.0 29.5 reduce-scatter.8
  673.7 71.7 reduce-scatter.4
  850.0 42.6 reduce-scatter.10
